TPU v7x, 32 devices: a whole 2x2x4 slice. The times are simulated.
32 devices in a mesh: groups: 2 (over y), angle: 4 (over z), slab: 2 (over x), row: 2 (over core).
Axes of the slice: x: 2, y: 2, z: 4, core: 2. Of those that a mesh axis runs over, the one named last changes fastest.
Arguments:
- projections: bfloat16 [32, 256, 2048], P(('groups', 'angle'), ('slab', 'row')), parts along dimension 0, may hold values from -24 to 24
- tile_lists: int32 [32, 4, 2], P(('groups', 'angle'), ('slab', 'row')), parts along dimension 0, may hold values from 0 to 3, as said below
- band_weights: bfloat16 [32, 8, 32, 4], P(('groups', 'angle'), None, ('slab', 'row')), parts along dimension 0, may hold values from 0.099609375 to 1
- band_offsets: int32 [32, 8, 32], P(('groups', 'angle'), None, ('slab', 'row')), parts along dimension 0, may hold values from 0 to 124
Outputs:
- volume: float32 [16, 32, 2048], P(('groups', 'angle'), ('slab', 'row')), parts along dimension 0
There are 2 independent parts, one for each index of `groups`. A program takes and returns all parts, laid end to end along the dimension named above; each array names one. Nothing has to cross between parts.
Inputs may be any that keep to these rules, and one draw needn't show every extreme that they name: `tile_lists`: each list holds 2 consecutive tile numbers in increasing order, starting at 0 or at 2; within the 4 views of one angle sector, one slab group lists one tile in at most 2 views, and some group reaches that.
All inputs are finite; a program needn't handle non-finite values.
Results may differ from a plain program's by a relative error of at most 0.0035.
Values may be sent and summed in bfloat16 or wider, within the bound.
A program may use at most 64 MiB of HBM per device.

v0:
```python
import math

import jax
import jax.numpy as jnp
from jax import lax
from jax.sharding import PartitionSpec as P


def from_behind(block, axis, distance):
    devices = range(lax.axis_size(axis))
    route = [((i - distance) % len(devices), i) for i in devices]
    return lax.ppermute(block, axis, route)


def ramp_block(detector_cols, first_col, block_cols):
    row_pos = lax.broadcasted_iota(jnp.float32, (detector_cols, block_cols), 0)
    col_pos = lax.broadcasted_iota(jnp.float32, (detector_cols, block_cols), 1) + first_col
    distance = col_pos - row_pos
    parity = jnp.abs(distance) % 2.0
    safe_gap = jnp.where(distance == 0.0, 1.0, distance)
    taps = jnp.where(
        distance == 0.0,
        0.25,
        jnp.where(parity == 1.0, -1.0 / (math.pi * math.pi * safe_gap * safe_gap), 0.0),
    )
    return taps.astype(jnp.bfloat16)


def ramp_filter(projection):
    view_count, row_count, detector_cols = projection.shape
    flattened = projection.reshape(view_count * row_count, detector_cols)
    block_cols = min(detector_cols, 512)
    pieces = [
        jnp.dot(
            flattened,
            ramp_block(detector_cols, first_col, block_cols),
            preferred_element_type=jnp.float32,
        )
        for first_col in range(0, detector_cols, block_cols)
    ]
    return (
        jnp.concatenate(pieces, axis=1)
        .astype(jnp.bfloat16)
        .reshape(view_count, row_count, detector_cols)
    )


def body(projections, tile_lists, band_weights, band_offsets):
    filtered = ramp_filter(projections)
    view_count, tile_rows, detector_cols = filtered.shape
    picked = tile_lists[:, 0, :]
    needed = picked.shape[1]
    tile_count = lax.axis_size(("slab", "row"))
    gathered = lax.all_gather(filtered, ("slab", "row"), axis=1, tiled=True)
    stacked = gathered.reshape(view_count, tile_count, tile_rows, detector_cols)
    chosen = jnp.take_along_axis(stacked, picked[:, :, None, None], axis=1).reshape(
        view_count, needed * tile_rows, detector_cols
    )
    band_width = band_weights.shape[3]
    y_total = band_weights.shape[1]
    z_group = band_weights.shape[2]
    cycle_size = lax.axis_size("angle")
    y_block = y_total // cycle_size
    cycle_index = lax.axis_index("angle")
    positions = jnp.arange(needed * tile_rows, dtype=jnp.int32)

    def project(y_start, y_count, z_start, z_count):
        y_first = jnp.asarray(y_start)
        zero_index = jnp.int32(0)
        z_first = jnp.int32(z_start)
        weights = lax.dynamic_slice(
            band_weights,
            (zero_index, y_first, z_first, zero_index),
            (view_count, y_count, z_count, band_width),
        )
        offsets = lax.dynamic_slice(
            band_offsets, (zero_index, y_first, z_first), (view_count, y_count, z_count)
        )
        dense_rows = jnp.zeros((view_count, y_count, z_count, needed * tile_rows), jnp.float32)
        for offset_step in range(band_width):
            matched = positions[None, None, None, :] == offsets[..., None] + offset_step
            dense_rows = dense_rows + jnp.where(
                matched, weights[..., offset_step : offset_step + 1].astype(jnp.float32), 0.0
            )
        dense_rows = dense_rows.astype(jnp.bfloat16).reshape(
            view_count, y_count * z_count, needed * tile_rows
        )
        summed = jnp.einsum("vlp,vpu->lu", dense_rows, chosen, preferred_element_type=jnp.float32)
        return summed.reshape(y_count, z_count, detector_cols)

    def forward_block(step):
        return (cycle_index - step - 1) % cycle_size * y_block

    def advance_one(step, carried):
        moved = from_behind(carried, "angle", 1)
        return moved + project(forward_block(step), y_block, 0, z_group)

    total = lax.fori_loop(
        1, cycle_size, advance_one, project(forward_block(0), y_block, 0, z_group)
    )
    return total * (math.pi / (view_count * cycle_size))


def solution(mesh):
    placed = (
        P(("groups", "angle"), ("slab", "row"), None),
        P(("groups", "angle"), ("slab", "row"), None),
        P(("groups", "angle"), None, ("slab", "row"), None),
        P(("groups", "angle"), None, ("slab", "row")),
    )
    return jax.shard_map(
        body,
        mesh=mesh,
        in_specs=placed,
        out_specs=P(("groups", "angle"), ("slab", "row"), None),
        check_vma=False,
    )
```

profile of v0, /device:TPU:0, one launch (start us, length us, event | category | flops | bytes accessed | tf_op | source)
XLA Modules:
  0.0 103.0 jit_solution(13176569937331933833)
XLA Ops:
  6.6 1.2 %copy-done = bf16[4,64,2048]{2,1,0:T(8,128)(2,1)S(1)} copy-done((bf16[4,64,2048]{2,1,0:T(8,128)(2,1)S(1)}, bf16[4,64,2048]{2,1,0:T(8,128)(2,1)}, u32[]{:S(2)}) %copy-start) | copy-done | bytes 1048600
  7.8 4.4 %fusion.51 = bf16[512,256]{0,1:T(8,128)(2,1)S(1)} fusion(bf16[256,2048]{1,0:T(8,128)(2,1)S(1)} %bitcast.120), kind=kOutput, calls=%fused_computation.91 | convolution fusion | flops 554827776 | bytes 1310720 | tf_op jit(solution)/shard_map/dot_general | solution.py:34
  12.2 4.4 %fusion.60 = bf16[512,256]{0,1:T(8,128)(2,1)S(1)} fusion(bf16[256,2048]{1,0:T(8,128)(2,1)S(1)} %bitcast.117, f32[512]{0:T(512)S(1)} %iota_add_fusion), kind=kOutput, calls=%fused_computation.94 | convolution fusion | flops 554827776 | bytes 1312768 | tf_op jit(solution)/shard_map/dot_general | solution.py:34
  16.6 4.4 %fusion.57 = bf16[512,256]{0,1:T(8,128)(2,1)S(1)} fusion(bf16[256,2048]{1,0:T(8,128)(2,1)S(1)} %bitcast.118, f32[512]{0:T(512)S(1)} %iota_add_fusion.1), kind=kOutput, calls=%fused_computation.93 | convolution fusion | flops 554827776 | bytes 1312768 | tf_op jit(solution)/shard_map/dot_general | solution.py:34
  21.0 4.4 %fusion.54 = bf16[512,256]{0,1:T(8,128)(2,1)S(1)} fusion(bf16[256,2048]{1,0:T(8,128)(2,1)S(1)} %bitcast.119, f32[512]{0:T(512)S(1)} %iota_add_fusion.2), kind=kOutput, calls=%fused_computation.92 | convolution fusion | flops 554827776 | bytes 1312768 | tf_op jit(solution)/shard_map/dot_general | solution.py:34
  25.4 1.1 %pad_maximum_fusion = bf16[4,64,2048]{2,1,0:T(8,128)(2,1)} fusion(bf16[4,64,512]{2,1,0:T(8,128)(2,1)S(1)} %bitcast.124, bf16[4,64,512]{2,1,0:T(8,128)(2,1)S(1)} %bitcast.125, bf16[4,64,512]{2,1,0:T(8,128)(2,1)S(1)} %bitcast.126, bf16[4,64,512]{2,1,0:T(8,128)(2,1)S(1)} %bitcast.123), kind=kLoop, calls=%fused_computation.95 | loop fusion | flops 4194304 | bytes 2097152 | tf_op jit(solution)/shard_map/concatenate | solution.py:42
  26.6 0.1 copy.40
  26.8 0.1 broadcast_in_dim.216
  26.9 0.1 copy.41
  27.0 0.1 reshape.253
  27.2 0.1 reshape.244
  27.4 0.1 eq.290
  27.7 0.1 reshape.243
  27.9 0.1 eq.286
  28.0 0.1 reshape.242
  28.2 0.1 eq.280
  28.4 0.1 reshape.241
  28.6 35.4 %all-gather.2.cloned.1.call-done = bf16[4,256,2048]{2,1,0:T(8,128)(2,1)} async-done(((bf16[4,64,2048]{2,1,0:T(8,128)(2,1)}), bf16[4,256,2048]{2,1,0:T(8,128)(2,1)}) %all-gather.2.cloned.1.call-update) | async-done | bytes 4194320 | tf_op jit(solution)/shard_map/all_gather | solution.py:54
  63.9 2.9 %gather_fusion = bf16[8,64,2048]{2,1,0:T(8,128)(2,1)S(1)} fusion(bf16[4,4,64,2048]{3,2,1,0:T(8,128)(2,1)} %bitcast.122, s32[8]{0:T(128)S(1)} %reshape.253), kind=kCustom, calls=%fused_computation | custom fusion | bytes 4194368 | tf_op jit(solution)/shard_map/jit(take_along_axis)/gather | solution.py:56
  66.8 0.3 bitcast_select_fusion
  67.1 0.4 convolution_bitcast_fusion.1
  67.5 0.9 copy-done.1
  68.4 27.1 %while.17 = (s32[]{:T(128)}, f32[2,8,2048]{2,1,0:T(8,128)S(1)}, s32[]{:T(128)}, s32[4,8,8]{2,1,0:T(8,128)S(1)}, bf16[4,8,8,4]{2,3,1,0:T(4,128)(2,1)S(1)}, /*inde...) while((s32[]{:T(128)}, f32[2,8,2048]{2,1,0:T(8,128)S(1)}, ...), condition=%wide.region_1.2_spmd.clone.clone, body=%wide.region_0.1_spmd.clone.clone.sunk | while | flops 33685972 | bytes 2902440 | solution.py:98
  68.4 1.5 %collective-permute-start = (f32[2,8,2048]{2,1,0:T(8,128)S(1)}, f32[2,8,2048]{2,1,0:T(8,128)S(1)}, u32[]{:S(2)}, u32[]{:S(2)}) collective-permute-start(f32[2,8,2048]{2,1,0:T(8,128)S(1)} %get-tuple-element.349), channel_id=1, source_target_pairs={{12,0},{0,4},{4,8},{8,12},{13,1},{1,5},{5,9},{9,13},{14,2},{2,6},{... | collective-permute-start | bytes 393224 | tf_op jit(solution)/shard_map/while/body/eval_jaxpr/ppermute | solution.py:12
  70.5 0.1 reshape.305
  71.3 4.5 %collective-permute-done = f32[2,8,2048]{2,1,0:T(8,128)S(1)} collective-permute-done((f32[2,8,2048]{2,1,0:T(8,128)S(1)}, f32[2,8,2048]{2,1,0:T(8,128)S(1)}, u32[]{:S(2)}, u32[]{:S(2)}) %collective-permute-start) | collective-permute-done | bytes 131104 | tf_op jit(solution)/shard_map/while/body/eval_jaxpr/ppermute | solution.py:12
  75.9 2.0 %fusion.111 = f32[2,8,2048]{2,1,0:T(8,128)S(1)} fusion(f32[2,8,2048]{2,1,0:T(8,128)S(1)} %collective-permute-done, bf16[4,128,2048]{2,1,0:T(8,128)(2,1)} %get-tuple-element.369, f32[2,8,4]{1,2,0:T(4,128)S(1)} %copy.66, s32[2,8,4]{1,2,0:T(4,128)S(1)} %copy.67, f32[2,8,4]{1,2,0:T(4,128)S(1)} %copy.68, s32[2,8,4]{1,2,0:T(4,128)S(1)} %copy.69, ...), kind=kOutput, calls=%fused_computation.3.clone.1 | convolution fusion | flops 33685504 | bytes 2361344 | tf_op jit(solution)/shard_map/while/body/eval_jaxpr/vlp,vpu->lu/dot_general | solution.py:88
  79.4 5.3 %collective-permute-done = f32[2,8,2048]{2,1,0:T(8,128)S(1)} collective-permute-done((f32[2,8,2048]{2,1,0:T(8,128)S(1)}, f32[2,8,2048]{2,1,0:T(8,128)S(1)}, u32[]{:S(2)}, u32[]{:S(2)}) %collective-permute-start) | collective-permute-done | bytes 131104 | tf_op jit(solution)/shard_map/while/body/eval_jaxpr/ppermute | solution.py:12
  84.7 2.0 %fusion.111 = f32[2,8,2048]{2,1,0:T(8,128)S(1)} fusion(f32[2,8,2048]{2,1,0:T(8,128)S(1)} %collective-permute-done, bf16[4,128,2048]{2,1,0:T(8,128)(2,1)} %get-tuple-element.369, f32[2,8,4]{1,2,0:T(4,128)S(1)} %copy.66, s32[2,8,4]{1,2,0:T(4,128)S(1)} %copy.67, f32[2,8,4]{1,2,0:T(4,128)S(1)} %copy.68, s32[2,8,4]{1,2,0:T(4,128)S(1)} %copy.69, ...), kind=kOutput, calls=%fused_computation.3.clone.1 | convolution fusion | flops 33685504 | bytes 2361344 | tf_op jit(solution)/shard_map/while/body/eval_jaxpr/vlp,vpu->lu/dot_general | solution.py:88
  88.2 5.3 %collective-permute-done = f32[2,8,2048]{2,1,0:T(8,128)S(1)} collective-permute-done((f32[2,8,2048]{2,1,0:T(8,128)S(1)}, f32[2,8,2048]{2,1,0:T(8,128)S(1)}, u32[]{:S(2)}, u32[]{:S(2)}) %collective-permute-start) | collective-permute-done | bytes 131104 | tf_op jit(solution)/shard_map/while/body/eval_jaxpr/ppermute | solution.py:12
  93.5 2.0 %fusion.111 = f32[2,8,2048]{2,1,0:T(8,128)S(1)} fusion(f32[2,8,2048]{2,1,0:T(8,128)S(1)} %collective-permute-done, bf16[4,128,2048]{2,1,0:T(8,128)(2,1)} %get-tuple-element.369, f32[2,8,4]{1,2,0:T(4,128)S(1)} %copy.66, s32[2,8,4]{1,2,0:T(4,128)S(1)} %copy.67, f32[2,8,4]{1,2,0:T(4,128)S(1)} %copy.68, s32[2,8,4]{1,2,0:T(4,128)S(1)} %copy.69, ...), kind=kOutput, calls=%fused_computation.3.clone.1 | convolution fusion | flops 33685504 | bytes 2361344 | tf_op jit(solution)/shard_map/while/body/eval_jaxpr/vlp,vpu->lu/dot_general | solution.py:88
  95.5 0.7 broadcast_multiply_fusion
  (124 shorter events, 5.2 us)
Async XLA Ops:
  6.5 1.2 %copy-start = (bf16[4,64,2048]{2,1,0:T(8,128)(2,1)S(1)}, bf16[4,64,2048]{2,1,0:T(8,128)(2,1)}, u32[]{:S(2)}) copy-start(bf16[4,64,2048]{2,1,0:T(8,128)(2,1)} %param.6) | copy-start | bytes 3145732
  6.5 57.4 %all-gather.2.cloned.1.call-start = ((), (), s32[]{:S(2)}) async-start(), calls=%async_computation | async-start | bytes 5242880 | tf_op jit(solution)/shard_map/all_gather | solution.py:54
  21.0 5.6 %copy-start.4 = (s32[4,1,2]{0,2,1:T(2,128)S(1)}, s32[4,1,2]{0,2,1:T(2,128)}, u32[]{:S(2)}) copy-start(s32[4,1,2]{0,2,1:T(2,128)} %param.7) | copy-start | bytes 100
  21.0 6.1 %copy-start.2 = (bf16[4,8,8,4]{2,3,1,0:T(4,128)(2,1)S(1)}, bf16[4,8,8,4]{2,3,1,0:T(4,128)(2,1)}, u32[]{:S(2)}) copy-start(bf16[4,8,8,4]{2,3,1,0:T(4,128)(2,1)} %param.8) | copy-start | bytes 6148
  21.0 6.3 %copy-start.3 = (s32[4,8,8]{2,1,0:T(8,128)S(1)}, s32[4,8,8]{2,1,0:T(8,128)}, u32[]{:S(2)}) copy-start(s32[4,8,8]{2,1,0:T(8,128)} %param.9) | copy-start | bytes 3076
  67.1 1.4 %copy-start.1 = (bf16[4,128,2048]{2,1,0:T(8,128)(2,1)}, bf16[4,128,2048]{2,1,0:T(8,128)(2,1)S(1)}, u32[]{:S(2)}) copy-start(bf16[4,128,2048]{2,1,0:T(8,128)(2,1)S(1)} %bitcast_select_fusion) | copy-start | bytes 6291460
  68.4 7.4 %collective-permute-start = (f32[2,8,2048]{2,1,0:T(8,128)S(1)}, f32[2,8,2048]{2,1,0:T(8,128)S(1)}, u32[]{:S(2)}, u32[]{:S(2)}) collective-permute-start(f32[2,8,2048]{2,1,0:T(8,128)S(1)} %get-tuple-element.349), channel_id=1, source_target_pairs={{12,0},{0,4},{4,8},{8,12},{13,1},{1,5},{5,9},{9,13},{14,2},{2,6},{... | collective-permute-start | bytes 393224 | tf_op jit(solution)/shard_map/while/body/eval_jaxpr/ppermute | solution.py:12
  77.9 6.8 %collective-permute-start = (f32[2,8,2048]{2,1,0:T(8,128)S(1)}, f32[2,8,2048]{2,1,0:T(8,128)S(1)}, u32[]{:S(2)}, u32[]{:S(2)}) collective-permute-start(f32[2,8,2048]{2,1,0:T(8,128)S(1)} %get-tuple-element.349), channel_id=1, source_target_pairs={{12,0},{0,4},{4,8},{8,12},{13,1},{1,5},{5,9},{9,13},{14,2},{2,6},{... | collective-permute-start | bytes 393224 | tf_op jit(solution)/shard_map/while/body/eval_jaxpr/ppermute | solution.py:12
  86.7 6.8 %collective-permute-start = (f32[2,8,2048]{2,1,0:T(8,128)S(1)}, f32[2,8,2048]{2,1,0:T(8,128)S(1)}, u32[]{:S(2)}, u32[]{:S(2)}) collective-permute-start(f32[2,8,2048]{2,1,0:T(8,128)S(1)} %get-tuple-element.349), channel_id=1, source_target_pairs={{12,0},{0,4},{4,8},{8,12},{13,1},{1,5},{5,9},{9,13},{14,2},{2,6},{... | collective-permute-start | bytes 393224 | tf_op jit(solution)/shard_map/while/body/eval_jaxpr/ppermute | solution.py:12
Sparse Core Ops, SparseCore 0:
  26.7 37.1 all-gather.1
where the time goes:
time: 103 us
  waiting for transfers between devices  50.4 us (49%)
  matrix products  24.1 us (23%)
  between operations  13.5 us (13%)
  local copies, waits for them, and re-layouts  11 us (11%)
  other arithmetic  2.23 us (2%)
  starting transfers between devices  1.52 us (1%)
    all_gather x1, waiting for transfers between devices, body(): gathered = lax.all_gather(filtered, ('slab', 'row'), axis=1, tiled=True)  35.4 us
    dot_general x4, matrix products, ramp_filter(): jnp.dot(flattened, ramp_block(detector_cols, first_col, block_cols), pref...  17.6 us
    ppermute x3, waiting for transfers between devices, from_behind(): return lax.ppermute(block, axis, route)  15 us
    dot_general x4, matrix products, project(): jnp.einsum('vlp,vpu->lu', dense_rows, chosen, preferred_element_type=jnp....  6.52 us
    gather x3, local copies, waits for them, and re-layouts, body(): jnp.take_along_axis(stacked, picked[:, :, None, None], axis=1)  3.05 us
    broadcast_in_dim x48, local copies, waits for them, and re-layouts, project(): jnp.where(matched, weights[..., offset_step:offset_step + 1].astype(jnp.f...  2.76 us
    eq x48, local copies, waits for them, and re-layouts, project(): matched = positions[None, None, None, :] == offsets[..., None] + offset_step  2.74 us
    unnamed x10, local copies, waits for them, and re-layouts  2.12 us
  transfers between devices with their start and end apart: 4, of which 4 were waited for; matrix products, arithmetic and copies ran while one was open for 6% of the time, Pallas kernels for 0%

commit v1 on v0

--- a/solution.py
+++ b/solution.py
@@ -1,9 +1,250 @@
+import functools
 import math
 
 import jax
 import jax.numpy as jnp
+import ml_dtypes
+import numpy as np
 from jax import lax
+from jax.experimental import pallas as pl
+from jax.experimental.pallas import tpu as pltpu
 from jax.sharding import PartitionSpec as P
+
+MESH = pl.DeviceIdType.MESH
+CHUNK = 256
+
+
+def ramp_strip(detector_cols, width):
+    rows = np.arange(2 * detector_cols - width)[:, None]
+    gap = np.arange(width)[None, :] + (detector_cols - width) - rows
+    gap32 = np.where(gap == 0, 1, gap).astype(np.float32)
+    scale = np.float32(math.pi * math.pi)
+    odd = np.where(gap % 2 != 0, np.float32(-1.0) / (scale * gap32 * gap32), np.float32(0.0))
+    return np.where(gap == 0, np.float32(0.25), odd).astype(ml_dtypes.bfloat16)
+
+
+def fused_kernel(
+    angles, scale,
+    x_hbm, lists_hbm, weights_hbm, offsets_hbm, strip_hbm,
+    out_ref,
+    x_v, lists_v, weights_v, offsets_v, strip_v,
+    dense, wmat, keep, core_out, core_in, slab_out, slab_in, angle_out, angle_in,
+    load_sem, wsend_sem, wrecv_sem, csend_sem, crecv_sem, ssend_sem, srecv_sem, asend_sem, arecv_sem,
+):
+    views, tile_rows, cols = x_v.shape
+    ys, zs, band = weights_v.shape[1:]
+    lines = ys * zs
+    share = lines // angles
+    depth = views * tile_rows
+    chunks = cols // CHUNK
+    angle = lax.axis_index("angle")
+    slab = lax.axis_index("slab")
+    row = lax.axis_index("row")
+
+    barrier = pltpu.get_barrier_semaphore()
+    near = [
+        (1 - slab, 1 - row),
+        (slab, 1 - row),
+        (1 - slab, row),
+    ]
+    near_ids = [{"slab": s, "row": r} for s, r in near]
+    far_ids = [{"angle": lax.rem(angle + j, angles)} for j in range(1, angles)]
+    for device in near_ids + far_ids:
+        pl.semaphore_signal(barrier, inc=1, device_id=device, device_id_type=MESH)
+
+    loads = [
+        pltpu.make_async_copy(src, dst, load_sem.at[i])
+        for i, (src, dst) in enumerate(
+            [
+                (lists_hbm, lists_v),
+                (weights_hbm, weights_v),
+                (offsets_hbm, offsets_v),
+                (x_hbm, x_v),
+                (strip_hbm, strip_v),
+            ]
+        )
+    ]
+    for load in loads:
+        load.start()
+    for load in loads[:3]:
+        load.wait()
+
+    lane = lax.broadcasted_iota(jnp.int32, (lines, 2 * tile_rows), 1)
+    second = lane >= tile_rows
+    within = jnp.where(second, lane - tile_rows, lane)
+    same = lax.broadcasted_iota(jnp.int32, (zs, zs), 0) == lax.broadcasted_iota(jnp.int32, (zs, zs), 1)
+    first_row, taps = [], []
+    for v in range(views):
+        offs = offsets_v[v].astype(jnp.float32)
+        column = jnp.concatenate(
+            [
+                jnp.sum(jnp.where(same, offs[y : y + 1, :], 0.0), axis=1, keepdims=True)
+                for y in range(ys)
+            ],
+            axis=0,
+        )
+        start = lists_v[v].astype(jnp.float32)[:, 0:1] * float(tile_rows)
+        first_row.append(column + start)
+        taps.append(weights_v[v].astype(jnp.float32).reshape(lines, band))
+    places = near + [(slab, row)]
+    for pair in range(views // 2):
+        a, b = 2 * pair, 2 * pair + 1
+        pos = jnp.where(second, first_row[b], first_row[a])
+        tap = [jnp.where(second, taps[b][:, k : k + 1], taps[a][:, k : k + 1]) for k in range(band)]
+        for slot, (s, r) in enumerate(places):
+            gap = (within + (s * 2 + r) * tile_rows).astype(jnp.float32) - pos
+            total = jnp.zeros((lines, 2 * tile_rows), jnp.float32)
+            for k in range(band):
+                total = total + jnp.where(gap == float(k), tap[k], 0.0)
+            where = pl.ds(pair * 2 * tile_rows, 2 * tile_rows)
+            if slot < 3:
+                dense[slot, :, where] = total.astype(jnp.bfloat16)
+            else:
+                wmat[slot, :, where] = total.astype(jnp.bfloat16)
+
+    pl.semaphore_wait(barrier, len(near_ids) + len(far_ids))
+    wcopies = [
+        pltpu.make_async_remote_copy(
+            src_ref=dense.at[slot],
+            dst_ref=wmat.at[slot],
+            send_sem=wsend_sem.at[slot],
+            recv_sem=wrecv_sem.at[slot],
+            device_id=near_ids[slot],
+            device_id_type=MESH,
+        )
+        for slot in range(3)
+    ]
+    for copy in wcopies:
+        copy.start()
+    for load in loads[3:]:
+        load.wait()
+
+    def core_copy(c):
+        return pltpu.make_async_remote_copy(
+            src_ref=core_out.at[c], dst_ref=core_in.at[c],
+            send_sem=csend_sem.at[c], recv_sem=crecv_sem.at[c],
+            device_id=near_ids[1], device_id_type=MESH,
+        )
+
+    def slab_copy(c):
+        return pltpu.make_async_remote_copy(
+            src_ref=slab_out.at[c], dst_ref=slab_in.at[c],
+            send_sem=ssend_sem.at[c], recv_sem=srecv_sem.at[c],
+            device_id=near_ids[2], device_id_type=MESH,
+        )
+
+    def angle_copy(c, j):
+        there = pl.multiple_of(lax.rem(angle + j, angles) * share, share)
+        return pltpu.make_async_remote_copy(
+            src_ref=angle_out.at[c, pl.ds(there, share)], dst_ref=angle_in.at[c, j - 1],
+            send_sem=asend_sem.at[c, j - 1], recv_sem=arecv_sem.at[c, j - 1],
+            device_id=far_ids[j - 1], device_id_type=MESH,
+        )
+
+    def filter_chunk(c):
+        rows = pl.ds((chunks - 1 - c) * CHUNK, cols)
+        return jnp.dot(
+            x_v[...].reshape(depth, cols), strip_v[rows, :], preferred_element_type=jnp.float32
+        ).astype(jnp.bfloat16)
+
+    def project_chunk(c, filtered):
+        part = jnp.dot(
+            wmat[...].reshape(4 * lines, depth), filtered, preferred_element_type=jnp.float32
+        )
+        core_out[c] = part[: 2 * lines].astype(jnp.bfloat16)
+        core_copy(c).start()
+        keep[c] = part[2 * lines :]
+
+    def core_step(c):
+        core_copy(c).wait_recv()
+        slab_out[c] = (keep[c, :lines] + core_in[c, :lines].astype(jnp.float32)).astype(jnp.bfloat16)
+        slab_copy(c).start()
+        keep[c, lines:] = keep[c, lines:] + core_in[c, lines:].astype(jnp.float32)
+
+    def slab_step(c):
+        slab_copy(c).wait_recv()
+        total = keep[c, lines:] + slab_in[c].astype(jnp.float32)
+        angle_out[c] = total.astype(jnp.bfloat16)
+        for j in range(1, angles):
+            angle_copy(c, j).start()
+        keep[c, lines:] = total
+
+    def angle_step(c):
+        here = pl.multiple_of(angle * share, share)
+        total = keep[c, pl.ds(lines + here, share)]
+        for j in range(1, angles):
+            angle_copy(c, j).wait_recv()
+            total = total + angle_in[c, j - 1].astype(jnp.float32)
+        out_ref[:, :, c * CHUNK : (c + 1) * CHUNK] = (total * scale).reshape(
+            share // zs, zs, CHUNK
+        )
+
+    lead = 1
+    filtered = {}
+    for step in range(chunks + lead + 7):
+        if step < chunks:
+            filtered[step] = filter_chunk(step)
+        c = step - lead
+        if c == 0:
+            for copy in wcopies:
+                copy.wait_recv()
+        if 0 <= c < chunks:
+            project_chunk(c, filtered.pop(c))
+        for late, act in ((2, core_step), (4, slab_step), (7, angle_step)):
+            if 0 <= c - late + 0 < chunks:
+                act(c - late)
+    for copy in wcopies:
+        copy.wait_send()
+    for c in range(chunks):
+        core_copy(c).wait_send()
+        slab_copy(c).wait_send()
+        for j in range(1, angles):
+            angle_copy(c, j).wait_send()
+
+
+def fused_body(angles, projections, tile_lists, band_weights, band_offsets):
+    views, tile_rows, cols = projections.shape
+    ys, zs, band = band_weights.shape[1:]
+    lines = ys * zs
+    share = lines // angles
+    chunks = cols // CHUNK
+    strip = jnp.asarray(ramp_strip(cols, CHUNK))
+    bf16, f32 = jnp.bfloat16, jnp.float32
+    dma = pltpu.SemaphoreType.DMA
+    return pl.pallas_call(
+        functools.partial(fused_kernel, angles, math.pi / (views * angles)),
+        out_shape=jax.ShapeDtypeStruct((ys // angles, zs, cols), f32),
+        in_specs=[pl.BlockSpec(memory_space=pl.ANY)] * 5,
+        out_specs=pl.BlockSpec(memory_space=pltpu.VMEM),
+        scratch_shapes=[
+            pltpu.VMEM(projections.shape, bf16),
+            pltpu.VMEM(tile_lists.shape, jnp.int32),
+            pltpu.VMEM(band_weights.shape, bf16),
+            pltpu.VMEM(band_offsets.shape, jnp.int32),
+            pltpu.VMEM(strip.shape, bf16),
+            pltpu.VMEM((3, lines, views * tile_rows), bf16),
+            pltpu.VMEM((4, lines, views * tile_rows), bf16),
+            pltpu.VMEM((chunks, 2 * lines, CHUNK), f32),
+            pltpu.VMEM((chunks, 2 * lines, CHUNK), bf16),
+            pltpu.VMEM((chunks, 2 * lines, CHUNK), bf16),
+            pltpu.VMEM((chunks, lines, CHUNK), bf16),
+            pltpu.VMEM((chunks, lines, CHUNK), bf16),
+            pltpu.VMEM((chunks, lines, CHUNK), bf16),
+            pltpu.VMEM((chunks, angles - 1, share, CHUNK), bf16),
+            dma((5,)),
+            dma((3,)),
+            dma((3,)),
+            dma((chunks,)),
+            dma((chunks,)),
+            dma((chunks,)),
+            dma((chunks,)),
+            dma((chunks, angles - 1)),
+            dma((chunks, angles - 1)),
+        ],
+        compiler_params=pltpu.CompilerParams(
+            collective_id=0, has_side_effects=True, vmem_limit_bytes=40 * 1024 * 1024
+        ),
+    )(projections, tile_lists, band_weights, band_offsets, strip)
 
 
 def from_behind(block, axis, distance):
@@ -108,8 +349,9 @@
         P(("groups", "angle"), None, ("slab", "row"), None),
         P(("groups", "angle"), None, ("slab", "row")),
     )
+    small = (mesh.shape["angle"], mesh.shape["slab"], mesh.shape["row"]) == (4, 2, 2)
     return jax.shard_map(
-        body,
+        functools.partial(fused_body, mesh.shape["angle"]) if small else body,
         mesh=mesh,
         in_specs=placed,
         out_specs=P(("groups", "angle"), ("slab", "row"), None),

time: 103 us -> 31.2 us (0.30)
  waiting for transfers between devices: 50.4 us -> 0 us
  Pallas kernels: 0 us -> 24.9 us
  matrix products: 24.1 us -> 0 us
  between operations: 13.5 us -> 0.01 us
  local copies, waits for them, and re-layouts: 11 us -> 5.94 us
  other arithmetic: 2.23 us -> 0 us
  starting transfers between devices: 1.52 us -> 0 us
    all_gather x1 -> x0, waiting for transfers between devices: 35.4 us -> none  [body(): gathered = lax.all_gather(filtered, ('slab', 'row'), axis=1, tiled=True)]
    pallas_call x0 -> x1, Pallas kernels: none -> 24.9 us  [fused_body(): pl.pallas_call(functools.partial(fused_kernel, angles, math.pi / (views *...]
    dot_general x8 -> x0, matrix products: 24.1 us -> none  [the longest x4 17.6 us: ramp_filter(): jnp.dot(flattened, ramp_block(detector_cols, first_col, block_cols), pref...]
    ppermute x3 -> x0, waiting for transfers between devices: 15 us -> none  [from_behind(): return lax.ppermute(block, axis, route)]
    unnamed x10 -> x9, local copies, waits for them, and re-layouts: 2.12 us -> 5.94 us
    gather x3 -> x0, local copies, waits for them, and re-layouts: 3.05 us -> none  [body(): jnp.take_along_axis(stacked, picked[:, :, None, None], axis=1)]
    broadcast_in_dim x50 -> x0, local copies, waits for them, and re-layouts: 2.92 us -> none  [the longest x48 2.76 us: project(): jnp.where(matched, weights[..., offset_step:offset_step + 1].astype(jnp.f...]
    eq x48 -> x0, local copies, waits for them, and re-layouts: 2.74 us -> none  [project(): matched = positions[None, None, None, :] == offsets[..., None] + offset_step]
  transfers between devices with their start and end apart: 4 -> 0, of which waited for: 4 -> 0; matrix products, arithmetic and copies ran while one was open for 6% -> 0% of each run, Pallas kernels for 0% -> 0%
where the time goes in v1:
time: 31.2 us; the launch traced here: 30.9 us
  Pallas kernels  24.9 us (80%)
  local copies, waits for them, and re-layouts  5.94 us (19%)
    pallas_call x1, Pallas kernels, fused_body(): pl.pallas_call(functools.partial(fused_kernel, angles, math.pi / (views *...  24.9 us
    unnamed x9, local copies, waits for them, and re-layouts  5.94 us

profile of v1, /device:TPU:0, one launch (start us, length us, event | category | flops | bytes accessed | tf_op | source)
XLA Modules:
  0.0 30.9 jit_solution(16650265344984322653)
XLA Ops:
  0.0 0.8 %copy.6.lists_hbm = s32[4,1,2]{2,1,0:T(1,128)S(1)} copy(s32[4,1,2]{0,2,1:T(2,128)} %param.6) | data formatting | bytes 64 | tf_op args[1]
  0.8 1.0 %copy.7.weights_hbm = bf16[4,8,8,4]{3,2,1,0:T(8,128)(2,1)S(1)} copy(bf16[4,8,8,4]{2,3,1,0:T(4,128)(2,1)} %param.7) | data formatting | bytes 4096 | tf_op args[2]
  1.8 0.0 copy-start
  1.8 1.5 %copy-done = bf16[3840,256]{1,0:T(8,128)(2,1)S(1)} copy-done((bf16[3840,256]{1,0:T(8,128)(2,1)S(1)}, bf16[3840,256]{1,0:T(8,128)(2,1)}, u32[]{:S(2)}) %copy-start) | copy-done | bytes 1966104
  3.3 0.0 copy-start.1
  3.3 1.2 %copy-done.1 = bf16[4,64,2048]{2,1,0:T(8,128)(2,1)S(1)} copy-done((bf16[4,64,2048]{2,1,0:T(8,128)(2,1)S(1)}, bf16[4,64,2048]{2,1,0:T(8,128)(2,1)}, u32[]{:S(2)}) %copy-start.1) | copy-done | bytes 1048600
  4.6 0.0 copy-start.2
  4.6 0.7 %copy-done.2 = s32[4,8,8]{2,1,0:T(8,128)S(1)} copy-done((s32[4,8,8]{2,1,0:T(8,128)S(1)}, s32[4,8,8]{2,1,0:T(8,128)}, u32[]{:S(2)}) %copy-start.2) | copy-done | bytes 1048
  5.3 24.9 %shard_map.55 = f32[2,8,2048]{2,1,0:T(8,128)S(1)} custom-call(bf16[4,64,2048]{2,1,0:T(8,128)(2,1)S(1)} %copy-done.1, s32[4,1,2]{2,1,0:T(1,128)S(1)} %copy.6.lists_hbm, bf16[4,8,8,4]{3,2,1,0:T(8,128)(2,1)S(1)} %copy.7.weights_hbm, s32[4,8,8]{2,1,0:T(8,128)S(1)} %copy-done.2, bf16[3840,256]{1,0:T(8,128)(2,1)S(1)} %copy-done), custom_call_target="tpu_custom_call" | custom-call | tf_op jit(solution)/shard_map/pallas_call | solution.py:214
  30.2 0.7 %copy.9 = f32[2,8,2048]{2,1,0:T(8,128)} copy(f32[2,8,2048]{2,1,0:T(8,128)S(1)} %shard_map.55) | data formatting | bytes 262144
Async XLA Ops:
  1.8 1.5 %copy-start = (bf16[3840,256]{1,0:T(8,128)(2,1)S(1)}, bf16[3840,256]{1,0:T(8,128)(2,1)}, u32[]{:S(2)}) copy-start(bf16[3840,256]{1,0:T(8,128)(2,1)} %constant.2.clone.strip_hbm) | copy-start | bytes 5898244
  3.3 1.2 %copy-start.1 = (bf16[4,64,2048]{2,1,0:T(8,128)(2,1)S(1)}, bf16[4,64,2048]{2,1,0:T(8,128)(2,1)}, u32[]{:S(2)}) copy-start(bf16[4,64,2048]{2,1,0:T(8,128)(2,1)} %x_hbm.1) | copy-start | bytes 3145732
  4.6 0.7 %copy-start.2 = (s32[4,8,8]{2,1,0:T(8,128)S(1)}, s32[4,8,8]{2,1,0:T(8,128)}, u32[]{:S(2)}) copy-start(s32[4,8,8]{2,1,0:T(8,128)} %offsets_hbm.1) | copy-start | bytes 3076

commit v2 on v1

v2 whole, which is shorter than its diff:
```python
import functools
import math

import jax
import jax.numpy as jnp
import ml_dtypes
import numpy as np
from jax import lax
from jax.experimental import pallas as pl
from jax.experimental.pallas import tpu as pltpu
from jax.sharding import PartitionSpec as P

MESH = pl.DeviceIdType.MESH
BLOCK = 256
WIDTHS = (512, 512, 512, 512)


def ramp_strip(detector_cols, width):
    rows = np.arange(2 * detector_cols - width)[:, None]
    gap = np.arange(width)[None, :] + (detector_cols - width) - rows
    gap32 = np.where(gap == 0, 1, gap).astype(np.float32)
    scale = np.float32(math.pi * math.pi)
    odd = np.where(gap % 2 != 0, np.float32(-1.0) / (scale * gap32 * gap32), np.float32(0.0))
    return np.where(gap == 0, np.float32(0.25), odd).astype(ml_dtypes.bfloat16)


def fused_kernel(
    angles, widths,
    x_hbm, lists_hbm, weights_hbm, offsets_hbm, strip_hbm,
    out_ref,
    x_v, lists_v, weights_v, offsets_v, strip_v,
    tables, wmat, filtered, keep, core_out, core_in, slab_out, slab_in, pair_out, pair_in, cross_out, cross_in,
    load_sem, tsend_sem, trecv_sem, csend_sem, crecv_sem, ssend_sem, srecv_sem, asend_sem, arecv_sem,
):
    views, tile_rows, cols = x_v.shape
    ys, band, zs = weights_v.shape[1:]
    lines = ys * zs
    share = lines // angles
    depth = views * tile_rows
    chunks = len(widths)
    firsts = [sum(widths[:c]) for c in range(chunks)]
    taps_wide = views * ys * band
    angle = lax.axis_index("angle")
    slab = lax.axis_index("slab")
    row = lax.axis_index("row")

    barrier = pltpu.get_barrier_semaphore()
    near_ids = [
        {"slab": 1 - slab, "row": 1 - row},
        {"slab": slab, "row": 1 - row},
        {"slab": 1 - slab, "row": row},
    ]
    half, parity = angle // 2, lax.rem(angle, 2)
    far_ids = [{"angle": 2 * half + 1 - parity}, {"angle": 2 * (1 - half) + parity}]
    for device in near_ids + far_ids:
        pl.semaphore_signal(barrier, inc=1, device_id=device, device_id_type=MESH)

    loads = [
        pltpu.make_async_copy(src, dst, load_sem.at[i])
        for i, (src, dst) in enumerate(
            [
                (lists_hbm, lists_v),
                (weights_hbm, weights_v),
                (offsets_hbm, offsets_v),
                (x_hbm, x_v),
                (strip_hbm, strip_v),
            ]
        )
    ]
    for load in loads:
        load.start()
    for load in loads[:3]:
        load.wait()

    same = lax.broadcasted_iota(jnp.int32, (zs, zs), 0) == lax.broadcasted_iota(jnp.int32, (zs, zs), 1)
    same = same.astype(jnp.float32).astype(jnp.bfloat16)

    def upright(pieces):
        flat = jnp.concatenate(pieces, axis=0).astype(jnp.bfloat16)
        return lax.dot_general(
            same, flat, (((1,), (1,)), ((), ())), preferred_element_type=jnp.float32
        )

    tables[3, :, :taps_wide] = upright(
        [weights_v[v, y].astype(jnp.float32) for v in range(views) for y in range(ys)]
    )
    spare = tables.shape[2] - taps_wide
    first_rows = upright(
        [offsets_v[v].astype(jnp.float32) for v in range(views)]
        + [jnp.zeros((spare - views * ys, zs), jnp.float32)]
    )
    lane = lax.broadcasted_iota(jnp.int32, (zs, spare), 1)
    for v in range(views):
        start = lists_v[0].astype(jnp.float32)[0:1, v : v + 1] * float(tile_rows)
        first_rows = first_rows + jnp.where((lane >= v * ys) & (lane < (v + 1) * ys), start, 0.0)
    tables[3, :, taps_wide:] = first_rows

    pl.semaphore_wait(barrier, len(near_ids) + len(far_ids))
    tcopies = [
        pltpu.make_async_remote_copy(
            src_ref=tables.at[3], dst_ref=tables.at[slot],
            send_sem=tsend_sem.at[slot], recv_sem=trecv_sem.at[slot],
            device_id=near_ids[slot], device_id_type=MESH,
        )
        for slot in range(3)
    ]
    for copy in tcopies:
        copy.start()
    for load in loads[3:]:
        load.wait()

    def build_bands():
        wide = (lines, 2 * tile_rows)
        lane = lax.broadcasted_iota(jnp.int32, wide, 1)
        second = lane >= tile_rows
        place = jnp.where(second, lane - tile_rows, lane) + (slab * 2 + row) * tile_rows
        place = place.astype(jnp.float32)

        def stretch(table, first, stride):
            return jnp.concatenate(
                [
                    jnp.broadcast_to(
                        table[:, first + y * stride : first + y * stride + 1], (zs, 2 * tile_rows)
                    )
                    for y in range(ys)
                ],
                axis=0,
            )

        for slot in range(4):
            table = tables[slot]
            for pair in range(views // 2):
                a, b = 2 * pair, 2 * pair + 1
                gap = place - jnp.where(
                    second,
                    stretch(table, taps_wide + b * ys, 1),
                    stretch(table, taps_wide + a * ys, 1),
                )
                total = jnp.zeros(wide, jnp.float32)
                for k in range(band):
                    tap = jnp.where(
                        second,
                        stretch(table, b * ys * band + k, band),
                        stretch(table, a * ys * band + k, band),
                    )
                    total = total + jnp.where(gap == float(k), tap, 0.0)
                where = pl.ds(pair * 2 * tile_rows, 2 * tile_rows)
                wmat[slot, :, where] = total.astype(jnp.bfloat16)

    def core_copy(c):
        return pltpu.make_async_remote_copy(
            src_ref=core_out[c], dst_ref=core_in[c],
            send_sem=csend_sem.at[c], recv_sem=crecv_sem.at[c],
            device_id=near_ids[1], device_id_type=MESH,
        )

    def slab_copy(c):
        return pltpu.make_async_remote_copy(
            src_ref=slab_out[c], dst_ref=slab_in[c],
            send_sem=ssend_sem.at[c], recv_sem=srecv_sem.at[c],
            device_id=near_ids[2], device_id_type=MESH,
        )

    def pair_copy(c):
        return pltpu.make_async_remote_copy(
            src_ref=pair_out[c].at[:, 1 - parity], dst_ref=pair_in[c],
            send_sem=asend_sem.at[c, 0], recv_sem=arecv_sem.at[c, 0],
            device_id=far_ids[0], device_id_type=MESH,
        )

    def cross_copy(c):
        return pltpu.make_async_remote_copy(
            src_ref=cross_out[c], dst_ref=cross_in[c],
            send_sem=asend_sem.at[c, 1], recv_sem=arecv_sem.at[c, 1],
            device_id=far_ids[1], device_id_type=MESH,
        )

    def filter_chunk(c):
        x = x_v[...].reshape(depth, cols)
        for at in range(0, widths[c], BLOCK):
            filtered[c][:, at : at + BLOCK] = jnp.dot(
                x,
                strip_v[pl.ds(cols - BLOCK - firsts[c] - at, cols), :],
                preferred_element_type=jnp.float32,
            ).astype(jnp.bfloat16)

    def project_chunk(c):
        part = jnp.dot(
            wmat[...].reshape(4 * lines, depth), filtered[c][...], preferred_element_type=jnp.float32
        )
        core_out[c][...] = part[: 2 * lines].astype(jnp.bfloat16)
        core_copy(c).start()
        keep[c][...] = part[2 * lines :]

    def core_step(c):
        core_copy(c).wait_recv()
        slab_out[c][...] = (keep[c][:lines] + core_in[c][:lines].astype(jnp.float32)).astype(jnp.bfloat16)
        slab_copy(c).start()
        keep[c][lines:] = keep[c][lines:] + core_in[c][lines:].astype(jnp.float32)

    def slab_step(c):
        slab_copy(c).wait_recv()
        total = keep[c][lines:] + slab_in[c][...].astype(jnp.float32)
        pair_out[c][...] = total.astype(jnp.bfloat16).reshape(2, 2, share, widths[c])
        pair_copy(c).start()
        keep[c][lines:] = total

    def pair_sum(c, other):
        first = pl.multiple_of(lines + (2 * other + parity) * share, share)
        return keep[c][pl.ds(first, share)] + pair_in[c][other].astype(jnp.float32)

    def pair_step(c):
        pair_copy(c).wait_recv()
        cross_out[c][...] = pair_sum(c, 1 - half).astype(jnp.bfloat16)
        cross_copy(c).start()

    def cross_step(c):
        cross_copy(c).wait_recv()
        total = pair_sum(c, half) + cross_in[c][...].astype(jnp.float32)
        out_ref[:, :, firsts[c] : firsts[c] + widths[c]] = total.reshape(share // zs, zs, widths[c])

    for c in range(chunks):
        filter_chunk(c)
    for copy in tcopies:
        copy.wait_recv()
    build_bands()
    for c in range(chunks):
        project_chunk(c)
    for c in range(chunks):
        core_step(c)
    for step in range(chunks + 1):
        if step < chunks:
            slab_step(step)
        if step >= 1:
            pair_step(step - 1)
    for c in range(chunks):
        cross_step(c)
    for copy in tcopies:
        copy.wait_send()
    for c in range(chunks):
        core_copy(c).wait_send()
        slab_copy(c).wait_send()
        pair_copy(c).wait_send()
        cross_copy(c).wait_send()


def fused_body(angles, projections, tile_lists, band_weights, band_offsets):
    views, tile_rows, cols = projections.shape
    ys, zs, band = band_weights.shape[1:]
    lines = ys * zs
    share = lines // angles
    widths = WIDTHS
    chunks = len(widths)
    strip = jnp.asarray(ramp_strip(cols, BLOCK))
    tile_lists = jnp.transpose(tile_lists, (1, 2, 0))
    band_weights = jnp.transpose(band_weights, (0, 1, 3, 2))
    table_wide = views * ys * band + -(-views * ys // 128) * 128
    bf16, f32 = jnp.bfloat16, jnp.float32
    dma = pltpu.SemaphoreType.DMA
    total = pl.pallas_call(
        functools.partial(fused_kernel, angles, widths),
        out_shape=jax.ShapeDtypeStruct((ys // angles, zs, cols), f32),
        in_specs=[pl.BlockSpec(memory_space=pl.ANY)] * 5,
        out_specs=pl.BlockSpec(memory_space=pltpu.VMEM),
        scratch_shapes=[
            pltpu.VMEM(projections.shape, bf16),
            pltpu.VMEM(tile_lists.shape, jnp.int32),
            pltpu.VMEM(band_weights.shape, bf16),
            pltpu.VMEM(band_offsets.shape, jnp.int32),
            pltpu.VMEM(strip.shape, bf16),
            pltpu.VMEM((4, zs, table_wide), f32),
            pltpu.VMEM((4, lines, views * tile_rows), bf16),
            [pltpu.VMEM((views * tile_rows, w), bf16) for w in widths],
            [pltpu.VMEM((2 * lines, w), f32) for w in widths],
            [pltpu.VMEM((2 * lines, w), bf16) for w in widths],
            [pltpu.VMEM((2 * lines, w), bf16) for w in widths],
            [pltpu.VMEM((lines, w), bf16) for w in widths],
            [pltpu.VMEM((lines, w), bf16) for w in widths],
            [pltpu.VMEM((2, 2, share, w), bf16) for w in widths],
            [pltpu.VMEM((2, share, w), bf16) for w in widths],
            [pltpu.VMEM((share, w), bf16) for w in widths],
            [pltpu.VMEM((share, w), bf16) for w in widths],
            dma((5,)),
            dma((3,)),
            dma((3,)),
            dma((chunks,)),
            dma((chunks,)),
            dma((chunks,)),
            dma((chunks,)),
            dma((chunks, 2)),
            dma((chunks, 2)),
        ],
        compiler_params=pltpu.CompilerParams(
            collective_id=0, has_side_effects=True, vmem_limit_bytes=65000 * 1024
        ),
    )(projections, tile_lists, band_weights, band_offsets, strip)
    return total * (math.pi / (views * angles))


def from_behind(block, axis, distance):
    devices = range(lax.axis_size(axis))
    route = [((i - distance) % len(devices), i) for i in devices]
    return lax.ppermute(block, axis, route)


def ramp_block(detector_cols, first_col, block_cols):
    row_pos = lax.broadcasted_iota(jnp.float32, (detector_cols, block_cols), 0)
    col_pos = lax.broadcasted_iota(jnp.float32, (detector_cols, block_cols), 1) + first_col
    distance = col_pos - row_pos
    parity = jnp.abs(distance) % 2.0
    safe_gap = jnp.where(distance == 0.0, 1.0, distance)
    taps = jnp.where(
        distance == 0.0,
        0.25,
        jnp.where(parity == 1.0, -1.0 / (math.pi * math.pi * safe_gap * safe_gap), 0.0),
    )
    return taps.astype(jnp.bfloat16)


def ramp_filter(projection):
    view_count, row_count, detector_cols = projection.shape
    flattened = projection.reshape(view_count * row_count, detector_cols)
    block_cols = min(detector_cols, 512)
    pieces = [
        jnp.dot(
            flattened,
            ramp_block(detector_cols, first_col, block_cols),
            preferred_element_type=jnp.float32,
        )
        for first_col in range(0, detector_cols, block_cols)
    ]
    return (
        jnp.concatenate(pieces, axis=1)
        .astype(jnp.bfloat16)
        .reshape(view_count, row_count, detector_cols)
    )


def body(projections, tile_lists, band_weights, band_offsets):
    filtered = ramp_filter(projections)
    view_count, tile_rows, detector_cols = filtered.shape
    picked = tile_lists[:, 0, :]
    needed = picked.shape[1]
    tile_count = lax.axis_size(("slab", "row"))
    gathered = lax.all_gather(filtered, ("slab", "row"), axis=1, tiled=True)
    stacked = gathered.reshape(view_count, tile_count, tile_rows, detector_cols)
    chosen = jnp.take_along_axis(stacked, picked[:, :, None, None], axis=1).reshape(
        view_count, needed * tile_rows, detector_cols
    )
    band_width = band_weights.shape[3]
    y_total = band_weights.shape[1]
    z_group = band_weights.shape[2]
    cycle_size = lax.axis_size("angle")
    y_block = y_total // cycle_size
    cycle_index = lax.axis_index("angle")
    positions = jnp.arange(needed * tile_rows, dtype=jnp.int32)

    def project(y_start, y_count, z_start, z_count):
        y_first = jnp.asarray(y_start)
        zero_index = jnp.int32(0)
        z_first = jnp.int32(z_start)
        weights = lax.dynamic_slice(
            band_weights,
            (zero_index, y_first, z_first, zero_index),
            (view_count, y_count, z_count, band_width),
        )
        offsets = lax.dynamic_slice(
            band_offsets, (zero_index, y_first, z_first), (view_count, y_count, z_count)
        )
        dense_rows = jnp.zeros((view_count, y_count, z_count, needed * tile_rows), jnp.float32)
        for offset_step in range(band_width):
            matched = positions[None, None, None, :] == offsets[..., None] + offset_step
            dense_rows = dense_rows + jnp.where(
                matched, weights[..., offset_step : offset_step + 1].astype(jnp.float32), 0.0
            )
        dense_rows = dense_rows.astype(jnp.bfloat16).reshape(
            view_count, y_count * z_count, needed * tile_rows
        )
        summed = jnp.einsum("vlp,vpu->lu", dense_rows, chosen, preferred_element_type=jnp.float32)
        return summed.reshape(y_count, z_count, detector_cols)

    def forward_block(step):
        return (cycle_index - step - 1) % cycle_size * y_block

    def advance_one(step, carried):
        moved = from_behind(carried, "angle", 1)
        return moved + project(forward_block(step), y_block, 0, z_group)

    total = lax.fori_loop(
        1, cycle_size, advance_one, project(forward_block(0), y_block, 0, z_group)
    )
    return total * (math.pi / (view_count * cycle_size))


def solution(mesh):
    placed = (
        P(("groups", "angle"), ("slab", "row"), None),
        P(("groups", "angle"), ("slab", "row"), None),
        P(("groups", "angle"), None, ("slab", "row"), None),
        P(("groups", "angle"), None, ("slab", "row")),
    )
    small = (mesh.shape["angle"], mesh.shape["slab"], mesh.shape["row"]) == (4, 2, 2)
    return jax.shard_map(
        functools.partial(fused_body, mesh.shape["angle"]) if small else body,
        mesh=mesh,
        in_specs=placed,
        out_specs=P(("groups", "angle"), ("slab", "row"), None),
        check_vma=False,
    )
```

time: 31.2 us -> 27 us (0.87)
  local copies, waits for them, and re-layouts: 5.94 us -> 0 us
  other arithmetic: 0 us -> 1.57 us
    unnamed x9 -> x0, local copies, waits for them, and re-layouts: 5.94 us -> none
    mul x0 -> x1, other arithmetic: none -> 1.57 us  [fused_body(): return total * (math.pi / (views * angles))]
where the time goes in v2:
time: 27 us; the launch traced here: 26.8 us
  Pallas kernels  25.2 us (93%)
  other arithmetic  1.57 us (6%)
    pallas_call x1, Pallas kernels, fused_body(): pl.pallas_call(functools.partial(fused_kernel, angles, widths), out_shape...  25.2 us
    mul x1, other arithmetic, fused_body(): return total * (math.pi / (views * angles))  1.57 us

profile of v2, /device:TPU:0, one launch (start us, length us, event | category | flops | bytes accessed | tf_op | source)
XLA Modules:
  0.0 26.8 jit_solution(15157335526722444079)
XLA Ops:
  0.0 25.2 %shard_map.55 = f32[2,8,2048]{2,1,0:T(8,128)} custom-call(bf16[4,64,2048]{2,1,0:T(8,128)(2,1)} %x_hbm.1, s32[1,2,4]{2,1,0:T(2,128)} %bitcast.3, bf16[4,8,4,8]{3,2,1,0:T(4,128)(2,1)} %bitcast.2, s32[4,8,8]{2,1,0:T(8,128)} %offsets_hbm.1, bf16[3840,256]{1,0:T(8,128)(2,1)} %constant.4.clone.strip_hbm), custom_call_target="tpu_custom_call" | custom-call | tf_op jit(solution)/shard_map/pallas_call | solution.py:260
  25.2 1.6 %broadcast_multiply_fusion = f32[2,8,2048]{2,1,0:T(8,128)} fusion(f32[2,8,2048]{2,1,0:T(8,128)} %shard_map.55), kind=kLoop, calls=%fused_computation | loop fusion | flops 32768 | bytes 262144 | tf_op jit(solution)/shard_map/mul | solution.py:297

commit v3 on v2

--- a/solution.py
+++ b/solution.py
@@ -29,7 +29,7 @@
     x_hbm, lists_hbm, weights_hbm, offsets_hbm, strip_hbm,
     out_ref,
     x_v, lists_v, weights_v, offsets_v, strip_v,
-    tables, wmat, filtered, keep, core_out, core_in, slab_out, slab_in, pair_out, pair_in, cross_out, cross_in,
+    tables, wmat, filtered, keep, core_out, core_in, slab_out, slab_in, angle_out, angle_in,
     load_sem, tsend_sem, trecv_sem, csend_sem, crecv_sem, ssend_sem, srecv_sem, asend_sem, arecv_sem,
 ):
     views, tile_rows, cols = x_v.shape
@@ -50,8 +50,7 @@
         {"slab": slab, "row": 1 - row},
         {"slab": 1 - slab, "row": row},
     ]
-    half, parity = angle // 2, lax.rem(angle, 2)
-    far_ids = [{"angle": 2 * half + 1 - parity}, {"angle": 2 * (1 - half) + parity}]
+    far_ids = [{"angle": lax.rem(angle + j, angles)} for j in range(1, angles)]
     for device in near_ids + far_ids:
         pl.semaphore_signal(barrier, inc=1, device_id=device, device_id_type=MESH)
 
@@ -161,18 +160,12 @@
             device_id=near_ids[2], device_id_type=MESH,
         )
 
-    def pair_copy(c):
+    def angle_copy(c, j):
+        there = pl.multiple_of(lax.rem(angle + j, angles) * share, share)
         return pltpu.make_async_remote_copy(
-            src_ref=pair_out[c].at[:, 1 - parity], dst_ref=pair_in[c],
-            send_sem=asend_sem.at[c, 0], recv_sem=arecv_sem.at[c, 0],
-            device_id=far_ids[0], device_id_type=MESH,
-        )
-
-    def cross_copy(c):
-        return pltpu.make_async_remote_copy(
-            src_ref=cross_out[c], dst_ref=cross_in[c],
-            send_sem=asend_sem.at[c, 1], recv_sem=arecv_sem.at[c, 1],
-            device_id=far_ids[1], device_id_type=MESH,
+            src_ref=angle_out[c].at[pl.ds(there, share)], dst_ref=angle_in[c].at[j - 1],
+            send_sem=asend_sem.at[c, j - 1], recv_sem=arecv_sem.at[c, j - 1],
+            device_id=far_ids[j - 1], device_id_type=MESH,
         )
 
     def filter_chunk(c):
@@ -201,22 +194,17 @@
     def slab_step(c):
         slab_copy(c).wait_recv()
         total = keep[c][lines:] + slab_in[c][...].astype(jnp.float32)
-        pair_out[c][...] = total.astype(jnp.bfloat16).reshape(2, 2, share, widths[c])
-        pair_copy(c).start()
+        angle_out[c][...] = total.astype(jnp.bfloat16)
+        for j in range(1, angles):
+            angle_copy(c, j).start()
         keep[c][lines:] = total
 
-    def pair_sum(c, other):
-        first = pl.multiple_of(lines + (2 * other + parity) * share, share)
-        return keep[c][pl.ds(first, share)] + pair_in[c][other].astype(jnp.float32)
-
-    def pair_step(c):
-        pair_copy(c).wait_recv()
-        cross_out[c][...] = pair_sum(c, 1 - half).astype(jnp.bfloat16)
-        cross_copy(c).start()
-
-    def cross_step(c):
-        cross_copy(c).wait_recv()
-        total = pair_sum(c, half) + cross_in[c][...].astype(jnp.float32)
+    def angle_step(c):
+        here = pl.multiple_of(angle * share, share)
+        total = keep[c][pl.ds(lines + here, share)]
+        for j in range(1, angles):
+            angle_copy(c, j).wait_recv()
+            total = total + angle_in[c][j - 1].astype(jnp.float32)
         out_ref[:, :, firsts[c] : firsts[c] + widths[c]] = total.reshape(share // zs, zs, widths[c])
 
     for c in range(chunks):
@@ -228,20 +216,17 @@
         project_chunk(c)
     for c in range(chunks):
         core_step(c)
-    for step in range(chunks + 1):
-        if step < chunks:
-            slab_step(step)
-        if step >= 1:
-            pair_step(step - 1)
-    for c in range(chunks):
-        cross_step(c)
+    for c in range(chunks):
+        slab_step(c)
+    for c in range(chunks):
+        angle_step(c)
     for copy in tcopies:
         copy.wait_send()
     for c in range(chunks):
         core_copy(c).wait_send()
         slab_copy(c).wait_send()
-        pair_copy(c).wait_send()
-        cross_copy(c).wait_send()
+        for j in range(1, angles):
+            angle_copy(c, j).wait_send()
 
 
 def fused_body(angles, projections, tile_lists, band_weights, band_offsets):
@@ -276,10 +261,8 @@
             [pltpu.VMEM((2 * lines, w), bf16) for w in widths],
             [pltpu.VMEM((lines, w), bf16) for w in widths],
             [pltpu.VMEM((lines, w), bf16) for w in widths],
-            [pltpu.VMEM((2, 2, share, w), bf16) for w in widths],
-            [pltpu.VMEM((2, share, w), bf16) for w in widths],
-            [pltpu.VMEM((share, w), bf16) for w in widths],
-            [pltpu.VMEM((share, w), bf16) for w in widths],
+            [pltpu.VMEM((lines, w), bf16) for w in widths],
+            [pltpu.VMEM((angles - 1, share, w), bf16) for w in widths],
             dma((5,)),
             dma((3,)),
             dma((3,)),
@@ -287,8 +270,8 @@
             dma((chunks,)),
             dma((chunks,)),
             dma((chunks,)),
-            dma((chunks, 2)),
-            dma((chunks, 2)),
+            dma((chunks, angles - 1)),
+            dma((chunks, angles - 1)),
         ],
         compiler_params=pltpu.CompilerParams(
             collective_id=0, has_side_effects=True, vmem_limit_bytes=65000 * 1024

time: 27 us -> 24.5 us (0.907)
  Pallas kernels: 25.2 us -> 22.7 us
    pallas_call x1, Pallas kernels: 25.2 us -> 22.7 us  [fused_body(): pl.pallas_call(functools.partial(fused_kernel, angles, widths), out_shape...]
where the time goes in v3:
time: 24.5 us; the launch traced here: 24.3 us
  Pallas kernels  22.7 us (93%)
  other arithmetic  1.57 us (6%)
    pallas_call x1, Pallas kernels, fused_body(): pl.pallas_call(functools.partial(fused_kernel, angles, widths), out_shape...  22.7 us
    mul x1, other arithmetic, fused_body(): return total * (math.pi / (views * angles))  1.57 us

profile of v3, /device:TPU:0, one launch (start us, length us, event | category | flops | bytes accessed | tf_op | source)
XLA Modules:
  0.0 24.3 jit_solution(10666558398290932725)
XLA Ops:
  0.0 22.7 %shard_map.55 = f32[2,8,2048]{2,1,0:T(8,128)} custom-call(bf16[4,64,2048]{2,1,0:T(8,128)(2,1)} %x_hbm.1, s32[1,2,4]{2,1,0:T(2,128)} %bitcast.3, bf16[4,8,4,8]{3,2,1,0:T(4,128)(2,1)} %bitcast.2, s32[4,8,8]{2,1,0:T(8,128)} %offsets_hbm.1, bf16[3840,256]{1,0:T(8,128)(2,1)} %constant.4.clone.strip_hbm), custom_call_target="tpu_custom_call" | custom-call | tf_op jit(solution)/shard_map/pallas_call | solution.py:245
  22.7 1.6 %broadcast_multiply_fusion = f32[2,8,2048]{2,1,0:T(8,128)} fusion(f32[2,8,2048]{2,1,0:T(8,128)} %shard_map.55), kind=kLoop, calls=%fused_computation | loop fusion | flops 32768 | bytes 262144 | tf_op jit(solution)/shard_map/mul | solution.py:280

commit v4 on v3

--- a/solution.py
+++ b/solution.py
@@ -12,7 +12,7 @@
 
 MESH = pl.DeviceIdType.MESH
 BLOCK = 256
-WIDTHS = (512, 512, 512, 512)
+WIDTHS = (256, 512, 512, 512, 256)
 
 
 def ramp_strip(detector_cols, width):
@@ -212,10 +212,11 @@
     for copy in tcopies:
         copy.wait_recv()
     build_bands()
-    for c in range(chunks):
-        project_chunk(c)
-    for c in range(chunks):
-        core_step(c)
+    for step in range(chunks + 2):
+        if step < chunks:
+            project_chunk(step)
+        if step >= 2:
+            core_step(step - 2)
     for c in range(chunks):
         slab_step(c)
     for c in range(chunks):

time: 24.5 us -> 24.5 us (level)
  no operation moved by 1% of the time
where the time goes in v4:
time: 24.5 us; the launch traced here: 24.3 us
  Pallas kernels  22.7 us (93%)
  other arithmetic  1.57 us (6%)
    pallas_call x1, Pallas kernels, fused_body(): pl.pallas_call(functools.partial(fused_kernel, angles, widths), out_shape...  22.7 us
    mul x1, other arithmetic, fused_body(): return total * (math.pi / (views * angles))  1.57 us

profile of v4, /device:TPU:0, one launch (start us, length us, event | category | flops | bytes accessed | tf_op | source)
XLA Modules:
  0.0 24.3 jit_solution(13291374822122194329)
XLA Ops:
  0.0 22.7 %shard_map.55 = f32[2,8,2048]{2,1,0:T(8,128)} custom-call(bf16[4,64,2048]{2,1,0:T(8,128)(2,1)} %x_hbm.1, s32[1,2,4]{2,1,0:T(2,128)} %bitcast.3, bf16[4,8,4,8]{3,2,1,0:T(4,128)(2,1)} %bitcast.2, s32[4,8,8]{2,1,0:T(8,128)} %offsets_hbm.1, bf16[3840,256]{1,0:T(8,128)(2,1)} %constant.4.clone.strip_hbm), custom_call_target="tpu_custom_call" | custom-call | tf_op jit(solution)/shard_map/pallas_call | solution.py:246
  22.7 1.6 %broadcast_multiply_fusion = f32[2,8,2048]{2,1,0:T(8,128)} fusion(f32[2,8,2048]{2,1,0:T(8,128)} %shard_map.55), kind=kLoop, calls=%fused_computation | loop fusion | flops 32768 | bytes 262144 | tf_op jit(solution)/shard_map/mul | solution.py:281
